TPU v7x, 32 devices: a whole 2x2x4 slice. The times are simulated.
32 devices in a mesh: scene: 2 (over x), tok: 16 (over z, y, core).
Axes of the slice: x: 2, y: 2, z: 4, core: 2. Of those that a mesh axis runs over, the one named last changes fastest.
Arguments:
- tokens: bfloat16 [16384, 768], P(('scene', 'tok')), parts along dimension 0, may hold values from -6 to 6
- qkv_weight: bfloat16 [768, 2304], replicated, may hold values from -0.21875 to 0.21875
- w_gate: float32 [4, 192, 384], replicated, may hold values from -0.4375 to 0.4375
- w_up: float32 [4, 192, 384], replicated, may hold values from -0.4375 to 0.4375
- w_down: float32 [4, 384, 192], replicated, may hold values from -0.3125 to 0.3125
- view_kind: int32 [32], P('scene'), parts along dimension 0, may hold values from 0 to 1, as said below
Outputs:
- mixed: bfloat16 [16384, 768], P(('scene', 'tok')), parts along dimension 0
There are 2 independent parts, one for each index of `scene`. A program takes and returns all parts, laid end to end along the dimension named above; an argument that names none is the same for every part. Nothing has to cross between parts.
Inputs may be any that keep to these rules, and one draw needn't show every extreme that they name: `view_kind`: exactly 12 of the 16 views are input views.
All inputs are finite; a program needn't handle non-finite values.
Results may differ from a plain program's by a relative error of at most 0.03.
Values may be sent and summed in bfloat16 or wider, within the bound.
No kernel may reach another device: no remote copies, remote signals or barrier semaphores. Data moves between devices by JAX's collectives and lax.ppermute only.
A program may use at most 64 MiB of HBM per device.

v0:
```python
import jax
import jax.numpy as jnp
from jax import lax
from jax.sharding import PartitionSpec as P

VIEWS = 16
NS_STEPS = 5
coef_a = 3.4445
coef_b = -4.775
coef_c = 2.0315
step_size = 0.8


def newton(start):
    iterate = start
    for step in range(NS_STEPS):
        gram = jnp.einsum(
            "mik,mjk->mij", iterate, iterate, preferred_element_type=jnp.float32
        ).astype(jnp.bfloat16)
        square = jnp.einsum("mij,mjk->mik", gram, gram, preferred_element_type=jnp.float32)
        mixer = (coef_b * gram.astype(jnp.float32) + coef_c * square).astype(jnp.bfloat16)
        moved = jnp.einsum("mij,mjk->mik", mixer, iterate, preferred_element_type=jnp.float32)
        iterate = (coef_a * iterate.astype(jnp.float32) + moved).astype(jnp.bfloat16)
    return iterate


def shards(tokens, qkv_weight, w_gate, w_up, w_down, view_kind):
    rows, width = tokens.shape
    heads, head_dim, hidden_dim = w_gate.shape
    groups = lax.axis_size("tok")
    place = lax.axis_index("tok")
    view_rows = rows * groups // VIEWS
    owner = place * rows // view_rows
    flag = jnp.sum(jnp.where(jnp.arange(VIEWS, dtype=jnp.int32) == owner, view_kind, 0))
    proj = jnp.dot(tokens, qkv_weight, preferred_element_type=jnp.float32).astype(jnp.bfloat16)
    query = proj[:, :width].reshape(rows, heads, head_dim)
    keys = proj[:, width : 2 * width].reshape(rows, heads, head_dim)
    values = proj[:, 2 * width :].reshape(rows, heads, head_dim)
    masked = values * flag.astype(jnp.bfloat16)
    gate_b = w_gate.astype(jnp.bfloat16)
    up_b = w_up.astype(jnp.bfloat16)
    down_b = w_down.astype(jnp.bfloat16)
    gate = jnp.einsum("thd,hdf->thf", keys, gate_b, preferred_element_type=jnp.float32)
    upper = jnp.einsum("thd,hdf->thf", keys, up_b, preferred_element_type=jnp.float32)
    sig = jax.nn.sigmoid(gate)
    act = gate * sig
    hidden = (act * upper).astype(jnp.bfloat16)
    dhid = -jnp.einsum("the,hfe->thf", masked, down_b, preferred_element_type=jnp.float32)
    dgate = (dhid * upper * (sig * (1.0 + gate * (1.0 - sig)))).astype(jnp.bfloat16)
    dup = (dhid * act).astype(jnp.bfloat16)
    grad_gate = jnp.einsum("thd,thf->hdf", keys, dgate, preferred_element_type=jnp.float32)
    grad_up = jnp.einsum("thd,thf->hdf", keys, dup, preferred_element_type=jnp.float32)
    grad_down = -jnp.einsum("the,thf->hef", masked, hidden, preferred_element_type=jnp.float32)
    grads = jnp.concatenate([grad_gate, grad_up, grad_down], axis=0)
    total = lax.psum(grads, "tok")
    norms = jnp.sqrt(jnp.sum(total * total, axis=(1, 2)))
    start = (total / (norms + 1e-07)[:, None, None]).astype(jnp.bfloat16)
    ortho = newton(start)
    stacked = jnp.concatenate([w_gate, w_up, jnp.transpose(w_down, (0, 2, 1))], axis=0)
    fresh = (stacked - step_size * ortho.astype(jnp.float32)).astype(jnp.bfloat16)
    gate2 = jnp.einsum("thd,hdf->thf", query, fresh[:heads], preferred_element_type=jnp.float32)
    upper2 = jnp.einsum(
        "thd,hdf->thf", query, fresh[heads : 2 * heads], preferred_element_type=jnp.float32
    )
    hidden2 = (jax.nn.silu(gate2) * upper2).astype(jnp.bfloat16)
    result = jnp.einsum(
        "thf,hef->the", hidden2, fresh[2 * heads :], preferred_element_type=jnp.float32
    )
    return result.reshape(rows, width).astype(jnp.bfloat16)


def solution(mesh):
    placed = (P(("scene", "tok"), None), P(), P(), P(), P(), P("scene"))
    return jax.shard_map(
        shards, mesh=mesh, in_specs=placed, out_specs=P(("scene", "tok"), None), check_vma=False
    )
```

profile of v0, /device:TPU:0, one launch (start us, length us, event | category | flops | bytes accessed | tf_op | source)
XLA Modules:
  0.0 202.8 jit_solution(2150129931057547903)
XLA Ops:
  6.5 0.0 copy-start
  6.5 0.0 all-reduce.2.cloned.1.call-start
  6.5 1.4 fusion.39
  8.6 0.0 copy-done
  8.6 3.1 %convolution_convert_fusion = bf16[512,2304]{1,0:T(8,128)(2,1)S(1)} fusion(bf16[512,768]{1,0:T(8,128)(2,1)} %param.6, bf16[768,2304]{1,0:T(8,128)(2,1)S(1)} %copy-done), kind=kOutput, calls=%fused_computation | convolution fusion | flops 1813118976 | bytes 6684672 | tf_op jit(solution)/shard_map/dot_general | solution.py:35
  11.8 1.5 fusion.53
  13.3 2.3 %copy.17 = bf16[512,768]{0,1:T(8,128)(2,1)} copy(bf16[512,768]{1,0:T(8,128)(2,1)} %get-tuple-element.6) | data formatting | bytes 1572864 | tf_op jit(solution)/shard_map/mul | solution.py:39
  15.6 2.3 %copy.16 = bf16[512,768]{0,1:T(8,128)(2,1)} copy(bf16[512,768]{1,0:T(8,128)(2,1)} %get-tuple-element.7) | data formatting | bytes 1572864 | tf_op jit(solution)/shard_map/slice | solution.py:37
  17.9 0.0 copy-start.3
  17.9 0.0 copy-start.6
  17.9 2.5 %fusion.33 = f32[4,512,384]{2,1,0:T(8,128)S(1)} fusion(bf16[512,4,192]{0,2,1:T(8,128)(2,1)} %bitcast.110, f32[4,192,384]{2,1,0:T(8,128)} %param.8), kind=kOutput, calls=%fused_computation.59 | convolution fusion | flops 302284800 | bytes 5111808 | tf_op jit(solution)/shard_map/thd,hdf->thf/dot_general | solution.py:43
  20.4 0.0 copy-done.3
  20.4 0.0 copy-done.6
  20.4 0.0 copy-start.4
  20.4 0.0 copy-start.5
  20.4 0.8 fusion.35
  21.2 0.3 copy-done.4
  21.5 0.4 copy-done.5
  21.9 0.8 fusion.37
  22.7 1.1 fusion.20
  23.9 1.9 fusion.18
  25.7 1.1 fusion.14
  26.8 2.1 %pad_maximum_fusion = f32[12,192,384]{2,1,0:T(8,128)} fusion(f32[4,192,384]{2,1,0:T(8,128)S(1)} %fusion.20, f32[4,192,384]{2,1,0:T(8,128)S(1)} %fusion.14, f32[4,192,384]{2,1,0:T(8,128)S(1)} %fusion.18), kind=kLoop, calls=%fused_computation.3 | loop fusion | flops 1769472 | bytes 7077888 | tf_op jit(solution)/shard_map/concatenate | solution.py:54
  28.9 0.0 all-reduce.2.cloned.1.call-update
  28.9 2.3 %copy.18 = bf16[512,768]{0,1:T(8,128)(2,1)} copy(bf16[512,768]{1,0:T(8,128)(2,1)} %get-tuple-element.5) | data formatting | bytes 1572864 | tf_op jit(solution)/shard_map/slice | solution.py:36
  31.2 106.7 %all-reduce.2.cloned.1.call-done = f32[12,192,384]{2,1,0:T(8,128)} async-done(((f32[12,192,384]{2,1,0:T(8,128)}), f32[12,192,384]{2,1,0:T(8,128)}) %all-reduce.2.cloned.1.call-update) | async-done | bytes 3538960 | tf_op jit(solution)/shard_map/psum | solution.py:55
  138.0 0.0 copy-start.2
  138.0 2.5 %multiply_reduce_fusion = f32[12]{0:T(128)S(1)} fusion(f32[12,192,384]{2,1,0:T(8,128)} %all-reduce.2.cloned.1.call-done), kind=kLoop, calls=%fused_computation.10 | loop fusion | flops 1769460 | bytes 3538992 | tf_op jit(solution)/shard_map/reduce_sum | solution.py:56
  140.5 0.5 copy-done.2
  141.0 0.4 divide_convert_fusion
  141.5 0.0 copy-start.1
  141.5 1.2 copy-done.1
  142.7 1.8 convolution_convert_fusion.5
  144.5 5.5 %add_convert_fusion.4 = bf16[12,192,384]{2,1,0:T(8,128)(2,1)} fusion(bf16[12,192,384]{2,1,0:T(8,128)(2,1)} %copy-done.1, bf16[12,192,192]{2,1,0:T(8,128)(2,1)} %convolution_convert_fusion.5), kind=kOutput, calls=%fused_computation.8 | convolution fusion | flops 515358720 | bytes 4423680 | tf_op jit(solution)/shard_map/mij,mjk->mik/dot_general | solution.py:22
  150.0 3.8 %convolution_convert_fusion.4 = bf16[12,192,192]{2,1,0:T(8,128)(2,1)} fusion(bf16[12,192,384]{2,1,0:T(8,128)(2,1)} %add_convert_fusion.4), kind=kOutput, calls=%fused_computation.44 | convolution fusion | flops 340180992 | bytes 2654208 | tf_op jit(solution)/shard_map/mik,mjk->mij/dot_general | solution.py:17
  153.8 5.6 %add_convert_fusion.3 = bf16[12,192,384]{2,1,0:T(8,128)(2,1)} fusion(bf16[12,192,384]{2,1,0:T(8,128)(2,1)} %add_convert_fusion.4, bf16[12,192,192]{2,1,0:T(8,128)(2,1)} %convolution_convert_fusion.4), kind=kOutput, calls=%fused_computation.7 | convolution fusion | flops 515358720 | bytes 4423680 | tf_op jit(solution)/shard_map/mij,mjk->mik/dot_general | solution.py:22
  159.4 3.8 %convolution_convert_fusion.3 = bf16[12,192,192]{2,1,0:T(8,128)(2,1)} fusion(bf16[12,192,384]{2,1,0:T(8,128)(2,1)} %add_convert_fusion.3), kind=kOutput, calls=%fused_computation.43 | convolution fusion | flops 340180992 | bytes 2654208 | tf_op jit(solution)/shard_map/mik,mjk->mij/dot_general | solution.py:17
  163.2 5.5 %add_convert_fusion.2 = bf16[12,192,384]{2,1,0:T(8,128)(2,1)} fusion(bf16[12,192,384]{2,1,0:T(8,128)(2,1)} %add_convert_fusion.3, bf16[12,192,192]{2,1,0:T(8,128)(2,1)} %convolution_convert_fusion.3), kind=kOutput, calls=%fused_computation.6 | convolution fusion | flops 515358720 | bytes 4423680 | tf_op jit(solution)/shard_map/mij,mjk->mik/dot_general | solution.py:22
  168.7 3.8 %convolution_convert_fusion.2 = bf16[12,192,192]{2,1,0:T(8,128)(2,1)} fusion(bf16[12,192,384]{2,1,0:T(8,128)(2,1)} %add_convert_fusion.2), kind=kOutput, calls=%fused_computation.42 | convolution fusion | flops 340180992 | bytes 2654208 | tf_op jit(solution)/shard_map/mik,mjk->mij/dot_general | solution.py:17
  172.6 5.6 %add_convert_fusion.1 = bf16[12,192,384]{2,1,0:T(8,128)(2,1)} fusion(bf16[12,192,384]{2,1,0:T(8,128)(2,1)} %add_convert_fusion.2, bf16[12,192,192]{2,1,0:T(8,128)(2,1)} %convolution_convert_fusion.2), kind=kOutput, calls=%fused_computation.5 | convolution fusion | flops 515358720 | bytes 4423680 | tf_op jit(solution)/shard_map/mij,mjk->mik/dot_general | solution.py:22
  178.2 3.8 %convolution_convert_fusion.1 = bf16[12,192,192]{2,1,0:T(8,128)(2,1)} fusion(bf16[12,192,384]{2,1,0:T(8,128)(2,1)} %add_convert_fusion.1), kind=kOutput, calls=%fused_computation.41 | convolution fusion | flops 340180992 | bytes 2654208 | tf_op jit(solution)/shard_map/mik,mjk->mij/dot_general | solution.py:17
  182.0 6.7 %fusion = bf16[12,192,384]{2,1,0:T(8,128)(2,1)} fusion(f32[4,192,384]{2,1,0:T(8,128)} %bitcast.116, f32[4,192,384]{2,1,0:T(8,128)} %param.9, f32[4,192,384]{2,1,0:T(8,128)} %param.8, bf16[12,192,384]{2,1,0:T(8,128)(2,1)} %add_convert_fusion.1, bf16[12,192,192]{2,1,0:T(8,128)(2,1)} %convolution_convert_fusion.1), kind=kOutput, calls=%fused_computation.2 | convolution fusion | flops 520667136 | bytes 7962624 | tf_op jit(solution)/shard_map/mij,mjk->mik/dot_general | solution.py:22
  188.7 2.3 %fusion.54 = f32[4,384,512]{1,2,0:T(8,128)S(1)} fusion(bf16[12,192,384]{2,1,0:T(8,128)(2,1)} %fusion, bf16[512,4,192]{0,2,1:T(8,128)(2,1)} %bitcast.117), kind=kOutput, calls=%fused_computation.82 | convolution fusion | flops 301989888 | bytes 5701632 | tf_op jit(solution)/shard_map/thd,hdf->thf/dot_general | solution.py:61
  191.0 0.0 copy-done.7
  191.0 0.0 copy-done.8
  191.0 1.1 fusion.1
  192.1 1.6 convolution_convert_fusion.6
  193.7 2.3 %copy.20 = bf16[512,768]{1,0:T(8,128)(2,1)} copy(bf16[512,768]{0,1:T(8,128)(2,1)} %bitcast.119) | data formatting | bytes 1572864 | tf_op jit(solution)/shard_map/convert_element_type | solution.py:69
  (3 shorter events, 0.0 us)
Async XLA Ops:
  6.5 2.1 %copy-start = (bf16[768,2304]{1,0:T(8,128)(2,1)S(1)}, bf16[768,2304]{1,0:T(8,128)(2,1)}, u32[]{:S(2)}) copy-start(bf16[768,2304]{1,0:T(8,128)(2,1)} %param.7) | copy-start | bytes 10616836
  6.5 131.4 %all-reduce.2.cloned.1.call-start = ((), (), s32[]{:S(2)}) async-start(), calls=%async_computation | async-start | bytes 7077888 | tf_op jit(solution)/shard_map/psum | solution.py:55
  17.9 2.5 %copy-start.3 = (bf16[512,768]{0,1:T(8,128)(2,1)S(1)}, bf16[512,768]{0,1:T(8,128)(2,1)}, u32[]{:S(2)}) copy-start(bf16[512,768]{0,1:T(8,128)(2,1)} %copy.16) | copy-start | bytes 2359300
  17.9 2.5 %copy-start.6 = (f32[4,192,384]{2,1,0:T(8,128)S(1)}, f32[4,192,384]{2,1,0:T(8,128)}, u32[]{:S(2)}) copy-start(f32[4,192,384]{2,1,0:T(8,128)} %param.9) | copy-start | bytes 3538948
  20.4 1.1 copy-start.4
  20.4 1.5 copy-start.5
  138.0 3.1 %copy-start.2 = (f32[12,192,384]{2,1,0:T(8,128)S(1)}, f32[12,192,384]{2,1,0:T(8,128)}, u32[]{:S(2)}) copy-start(f32[12,192,384]{2,1,0:T(8,128)} %all-reduce.2.cloned.1.call-done) | copy-start | bytes 10616836
  141.5 1.2 copy-start.1
  188.7 2.3 %copy-start.7 = (bf16[512,768]{0,1:T(8,128)(2,1)S(1)}, bf16[512,768]{0,1:T(8,128)(2,1)}, u32[]{:S(2)}) copy-start(bf16[512,768]{0,1:T(8,128)(2,1)} %copy.18) | copy-start | bytes 2359300
  188.7 2.3 %copy-start.8 = (bf16[12,192,384]{2,1,0:T(8,128)(2,1)S(1)}, bf16[12,192,384]{2,1,0:T(8,128)(2,1)}, u32[]{:S(2)}) copy-start(bf16[12,192,384]{2,1,0:T(8,128)(2,1)} %fusion) | copy-start | bytes 5308420
Sparse Core Ops, SparseCore 0:
  29.0 108.8 all-reduce.1
where the time goes:
time: 203 us
  waiting for transfers between devices  107 us (53%)
  matrix products  62.4 us (31%)
  between operations  14.2 us (7%)
  local copies, waits for them, and re-layouts  11.6 us (6%)
  other arithmetic  7.94 us (4%)
    psum x1, waiting for transfers between devices, shards(): total = lax.psum(grads, 'tok')  107 us
    dot_general x5, matrix products, newton(): jnp.einsum('mij,mjk->mik', mixer, iterate, preferred_element_type=jnp.flo...  28.9 us
    dot_general x5, matrix products, newton(): jnp.einsum('mik,mjk->mij', iterate, iterate, preferred_element_type=jnp.f...  17.1 us
  transfers between devices with their start and end apart: 1, of which 1 were waited for; matrix products, arithmetic and copies ran while one was open for 1% of the time, Pallas kernels for 0%

commit v1 on v0

--- a/solution.py
+++ b/solution.py
@@ -52,7 +52,9 @@
     grad_up = jnp.einsum("thd,thf->hdf", keys, dup, preferred_element_type=jnp.float32)
     grad_down = -jnp.einsum("the,thf->hef", masked, hidden, preferred_element_type=jnp.float32)
     grads = jnp.concatenate([grad_gate, grad_up, grad_down], axis=0)
-    total = lax.psum(grads, "tok")
+    total = grads
+    for hop in (1, 2, 4, 8):
+        total = total + lax.ppermute(total, "tok", [(dev, dev ^ hop) for dev in range(16)])
     norms = jnp.sqrt(jnp.sum(total * total, axis=(1, 2)))
     start = (total / (norms + 1e-07)[:, None, None]).astype(jnp.bfloat16)
     ortho = newton(start)

time: 203 us -> 375 us (1.85)
  waiting for transfers between devices: 107 us -> 308 us
  matrix products: 62.4 us -> 43.5 us
  between operations: 14.2 us -> 0.83 us
  starting transfers between devices: 0.01 us -> 7.9 us
  local copies, waits for them, and re-layouts: 11.6 us -> 6.74 us
    ppermute x0 -> x4, waiting for transfers between devices: none -> 308 us  [shards(): lax.ppermute(total, 'tok', [(dev, dev ^ hop) for dev in range(16)])]
    psum x1 -> x0, waiting for transfers between devices: 107 us -> none  [shards(): total = lax.psum(grads, 'tok')]
    dot_general x5, matrix products: 28.9 us -> 19.6 us  [newton(): jnp.einsum('mij,mjk->mik', mixer, iterate, preferred_element_type=jnp.flo...]
    dot_general x5, matrix products: 17.1 us -> 9.15 us  [newton(): jnp.einsum('mik,mjk->mij', iterate, iterate, preferred_element_type=jnp.f...]
    ppermute x0 -> x4, starting transfers between devices: none -> 7.9 us  [shards(): lax.ppermute(total, 'tok', [(dev, dev ^ hop) for dev in range(16)])]
  transfers between devices with their start and end apart: 1 -> 4, of which waited for: 1 -> 4; matrix products, arithmetic and copies ran while one was open for 1% -> 1% of each run, Pallas kernels for 0% -> 0%
where the time goes in v1:
time: 375 us; the launch traced here: 374 us
  waiting for transfers between devices  308 us (82%)
  matrix products  43.5 us (12%)
  starting transfers between devices  7.9 us (2%)
  other arithmetic  7.08 us (2%)
  local copies, waits for them, and re-layouts  6.74 us (2%)
    ppermute x4, waiting for transfers between devices, shards(): lax.ppermute(total, 'tok', [(dev, dev ^ hop) for dev in range(16)])  308 us
    dot_general x5, matrix products, newton(): jnp.einsum('mij,mjk->mik', mixer, iterate, preferred_element_type=jnp.flo...  19.6 us
    dot_general x5, matrix products, newton(): jnp.einsum('mik,mjk->mij', iterate, iterate, preferred_element_type=jnp.f...  9.15 us
    ppermute x4, starting transfers between devices, shards(): lax.ppermute(total, 'tok', [(dev, dev ^ hop) for dev in range(16)])  7.9 us
  transfers between devices with their start and end apart: 4, of which 4 were waited for; matrix products, arithmetic and copies ran while one was open for 1% of the time, Pallas kernels for 0%

profile of v1, /device:TPU:0, one launch (start us, length us, event | category | flops | bytes accessed | tf_op | source)
XLA Modules:
  0.0 374.2 jit_solution(4084092790220239935)
XLA Ops:
  0.0 0.0 copy-start
  0.0 1.4 fusion.40
  2.1 0.0 copy-done
  2.1 3.1 convolution_convert_fusion
  5.3 1.0 fusion.55
  6.3 0.3 copy.17
  6.6 0.3 copy.16
  6.9 0.7 copy-done.5
  7.6 0.8 fusion.34
  8.4 0.4 copy-done.4
  8.8 0.8 fusion.36
  9.7 0.4 copy-done.2
  10.1 0.8 fusion.38
  10.9 1.1 fusion.20
  12.1 1.9 fusion.18
  13.9 1.1 fusion.14
  15.1 0.3 pad_maximum_fusion
  15.4 0.5 collective-permute-start
  15.9 5.8 %collective-permute-done = f32[12,192,384]{2,1,0:T(8,128)S(1)} collective-permute-done((f32[12,192,384]{2,1,0:T(8,128)S(1)}, f32[12,192,384]{2,1,0:T(8,128)S(1)}, u32[]{:S(2)}, u32[]{:S(2)}) %collective-permute-start) | collective-permute-done | bytes 3538976 | tf_op jit(solution)/shard_map/ppermute | solution.py:57
  21.7 0.5 fusion.54
  22.2 3.0 collective-permute-start.1
  25.1 76.8 %collective-permute-done.1 = f32[12,192,384]{2,1,0:T(8,128)S(1)} collective-permute-done((f32[12,192,384]{2,1,0:T(8,128)S(1)}, f32[12,192,384]{2,1,0:T(8,128)S(1)}, u32[]{:S(2)}, u32[]{:S(2)}) %collective-permute-start.1) | collective-permute-done | bytes 3538976 | tf_op jit(solution)/shard_map/ppermute | solution.py:57
  102.0 0.5 add.63
  102.5 1.9 collective-permute-start.2
  104.4 76.3 %collective-permute-done.2 = f32[12,192,384]{2,1,0:T(8,128)S(1)} collective-permute-done((f32[12,192,384]{2,1,0:T(8,128)S(1)}, f32[12,192,384]{2,1,0:T(8,128)S(1)}, u32[]{:S(2)}, u32[]{:S(2)}) %collective-permute-start.2) | collective-permute-done | bytes 3538976 | tf_op jit(solution)/shard_map/ppermute | solution.py:57
  180.6 0.4 add.64
  181.0 2.6 collective-permute-start.3
  183.6 2.3 copy.18
  185.9 149.2 %collective-permute-done.3 = f32[12,192,384]{2,1,0:T(8,128)} collective-permute-done((f32[12,192,384]{2,1,0:T(8,128)S(1)}, f32[12,192,384]{2,1,0:T(8,128)}, u32[]{:S(2)}, u32[]{:S(2)}) %collective-permute-start.3) | collective-permute-done | bytes 3538976 | tf_op jit(solution)/shard_map/ppermute | solution.py:57
  335.1 2.5 multiply_reduce_fusion
  337.6 0.4 divide_convert_fusion
  338.1 1.8 convolution_convert_fusion.5
  339.9 3.5 add_convert_fusion.4
  343.4 1.8 convolution_convert_fusion.4
  345.2 3.5 add_convert_fusion.3
  348.7 1.8 convolution_convert_fusion.3
  350.5 3.5 add_convert_fusion.2
  354.0 1.8 convolution_convert_fusion.2
  355.9 3.5 add_convert_fusion.1
  359.3 0.0 copy-start.3
  359.4 1.8 convolution_convert_fusion.1
  361.2 0.0 copy-done.3
  361.2 5.7 %fusion = bf16[12,192,384]{2,1,0:T(8,128)(2,1)} fusion(f32[4,192,384]{2,1,0:T(8,128)S(1)} %bitcast.116, f32[4,192,384]{2,1,0:T(8,128)} %param.9, f32[4,192,384]{2,1,0:T(8,128)} %param.8, bf16[12,192,384]{2,1,0:T(8,128)(2,1)S(1)} %add_convert_fusion.1, bf16[12,192,192]{2,1,0:T(8,128)(2,1)} %convolution_convert_fusion.1), kind=kOutput, calls=%fused_computation.2 | convolution fusion | flops 520667136 | bytes 7962624 | tf_op jit(solution)/shard_map/mij,mjk->mik/dot_general | solution.py:22
  366.9 2.3 fusion.56
  369.2 1.1 fusion.1
  370.3 0.0 copy-start.1
  370.3 1.6 convolution_convert_fusion.6
  371.9 2.3 copy.20
  (9 shorter events, 0.0 us)
Async XLA Ops:
  0.0 2.1 copy-start
  6.3 1.3 copy-start.5
  7.6 1.3 copy-start.4
  8.8 1.3 copy-start.2
  15.4 6.4 %collective-permute-start = (f32[12,192,384]{2,1,0:T(8,128)S(1)}, f32[12,192,384]{2,1,0:T(8,128)S(1)}, u32[]{:S(2)}, u32[]{:S(2)}) collective-permute-start(f32[12,192,384]{2,1,0:T(8,128)S(1)} %pad_maximum_fusion), channel_id=1, source_target_pairs={{0,1},{1,0},{2,3},{3,2},{4,5},{5,4},{6,7},{7,6},{8,9},{9,8},{10,11... | collective-permute-start | bytes 10616840 | tf_op jit(solution)/shard_map/ppermute | solution.py:57
  22.2 79.8 %collective-permute-start.1 = (f32[12,192,384]{2,1,0:T(8,128)S(1)}, f32[12,192,384]{2,1,0:T(8,128)S(1)}, u32[]{:S(2)}, u32[]{:S(2)}) collective-permute-start(f32[12,192,384]{2,1,0:T(8,128)S(1)} %fusion.54), channel_id=1, source_target_pairs={{0,2},{1,3},{2,0},{3,1},{4,6},{5,7},{6,4},{7,5},{8,10},{9,11},{10,... | collective-permute-start | bytes 10616840 | tf_op jit(solution)/shard_map/ppermute | solution.py:57
  102.5 78.1 %collective-permute-start.2 = (f32[12,192,384]{2,1,0:T(8,128)S(1)}, f32[12,192,384]{2,1,0:T(8,128)S(1)}, u32[]{:S(2)}, u32[]{:S(2)}) collective-permute-start(f32[12,192,384]{2,1,0:T(8,128)S(1)} %add.63), channel_id=1, source_target_pairs={{0,4},{1,5},{2,6},{3,7},{4,0},{5,1},{6,2},{7,3},{8,12},{9,13},{10,... | collective-permute-start | bytes 10616840 | tf_op jit(solution)/shard_map/ppermute | solution.py:57
  181.0 154.1 %collective-permute-start.3 = (f32[12,192,384]{2,1,0:T(8,128)S(1)}, f32[12,192,384]{2,1,0:T(8,128)}, u32[]{:S(2)}, u32[]{:S(2)}) collective-permute-start(f32[12,192,384]{2,1,0:T(8,128)S(1)} %add.64), channel_id=1, source_target_pairs={{0,8},{1,9},{2,10},{3,11},{4,12},{5,13},{6,14},{7,15},{8,0},{9,1},... | collective-permute-start | bytes 10616840 | tf_op jit(solution)/shard_map/ppermute | solution.py:57
  359.3 1.8 copy-start.3
  366.8 2.3 copy-start.6
  366.9 2.3 copy-start.7
  370.3 3.9 %copy-start.1 = (bf16[768,2304]{1,0:T(8,128)(2,1)S(1)}, bf16[768,2304]{1,0:T(8,128)(2,1)}, u32[]{:S(2)}) copy-start(bf16[768,2304]{1,0:T(8,128)(2,1)} %param.7) | copy-start | bytes 10616836
